TPU v7x, 32 devices: a whole 2x2x4 slice. The times are simulated.
32 devices in a mesh: parts: 2 (over y), seq: 8 (over z, x), head: 2 (over core).
Axes of the slice: x: 2, y: 2, z: 4, core: 2. Of those that a mesh axis runs over, the one named last changes fastest.
Arguments:
- queries: bfloat16 [2048, 4096], P(('parts', 'seq', 'head')), parts along dimension 0, may hold values from -0.59765625 to 0.59765625
- keys: bfloat16 [2048, 4096], P(('parts', 'seq', 'head')), parts along dimension 0, may hold values from -0.59765625 to 0.59765625
- values: bfloat16 [2048, 4096], P(('parts', 'seq', 'head')), parts along dimension 0, may hold values from -0.59765625 to 0.59765625
- out_grad: bfloat16 [2048, 4096], P(('parts', 'seq', 'head')), parts along dimension 0, may hold values from -0.59765625 to 0.59765625
- decay_log: bfloat16 [2048, 32], P(('parts', 'seq', 'head')), parts along dimension 0, may hold values from -1 to 0, as said below
Outputs:
- grad_q: bfloat16 [2048, 4096], P(('parts', 'seq', 'head')), parts along dimension 0
- grad_k: bfloat16 [2048, 4096], P(('parts', 'seq', 'head')), parts along dimension 0
- grad_v: bfloat16 [2048, 4096], P(('parts', 'seq', 'head')), parts along dimension 0
There are 2 independent parts, one for each index of `parts`. A program takes and returns all parts, laid end to end along the dimension named above; each array names one. Nothing has to cross between parts.
Inputs may be any that keep to these rules, and one draw needn't show every extreme that they name: `decay_log`: negative everywhere.
All inputs are finite; a program needn't handle non-finite values.
Results may differ from a plain program's by a relative error of at most 0.0058.
Values may be sent and summed in bfloat16 or wider, within the bound.
A program may use at most 64 MiB of HBM per device.

v0:
```python
import jax
import jax.numpy as jnp
from jax import lax
from jax.sharding import PartitionSpec as P

BLK = 64


def shifted(block, axis, distance):
    devices = range(lax.axis_size(axis))
    route = [(i - distance, i) for i in devices if i - distance in devices]
    return lax.ppermute(block, axis, route)


def block_parts(queries, keys, values, out_grad, decay_factor):
    cumul = jnp.cumsum(decay_factor.astype(jnp.float32), axis=1)
    ending = cumul[:, -1]
    keep = jnp.exp(ending[:, None] - cumul)
    rising = jnp.exp(cumul)
    weighted_v = (values * keep[..., None]).astype(jnp.bfloat16)
    kv_block = jnp.einsum("nthi,nthj->nhij", keys, weighted_v, preferred_element_type=jnp.float32)
    weighted_q = (queries * rising[..., None]).astype(jnp.bfloat16)
    qo_block = jnp.einsum(
        "nthi,nthj->nhij", weighted_q, out_grad, preferred_element_type=jnp.float32
    )
    trans = jnp.swapaxes(cumul, 1, 2)
    diff = trans[..., :, None] - trans[..., None, :]
    length = cumul.shape[1]
    lower = jnp.arange(length)[:, None] >= jnp.arange(length)[None, :]
    mask = jnp.where(lower, jnp.exp(jnp.minimum(diff, 0.0)), 0.0)
    vscore = (
        jnp.einsum("nthd,nshd->nhts", out_grad, values, preferred_element_type=jnp.float32) * mask
    ).astype(jnp.bfloat16)
    qscore = (
        jnp.einsum("nthd,nshd->nhts", queries, keys, preferred_element_type=jnp.float32) * mask
    ).astype(jnp.bfloat16)
    local_q = jnp.einsum("nhts,nshd->nthd", vscore, keys, preferred_element_type=jnp.float32)
    local_k = jnp.einsum("nhts,nthd->nshd", vscore, queries, preferred_element_type=jnp.float32)
    local_v = jnp.einsum("nhts,nthd->nshd", qscore, out_grad, preferred_element_type=jnp.float32)
    return (jnp.exp(ending), kv_block, qo_block, rising, keep, local_q, local_k, local_v)


def chain(earlier, later):
    return (earlier[0] * later[0], later[0][..., None, None] * earlier[1] + later[1])


def prepare(queries, keys, values, out_grad, decay_log):
    groups = decay_log.shape[1]
    depth = queries.shape[1] // groups
    blocks = decay_log.shape[0] // BLK

    def split_point(array):
        return array.reshape(blocks, BLK, groups, depth)

    inputs = (
        split_point(queries),
        split_point(keys),
        split_point(values),
        split_point(out_grad),
        decay_log.reshape(blocks, BLK, groups),
    )
    parts = block_parts(*inputs)
    factor, kv_block, qo_block = (parts[0], parts[1], parts[2])
    forward = (factor[0], kv_block[0])
    index = 1
    forward = chain(forward, (factor[index], kv_block[index]))
    backward = (factor[blocks - 1], qo_block[blocks - 1])
    index = 0
    backward = chain(backward, (factor[index], qo_block[index]))
    identity = (jnp.ones_like(factor[0]), jnp.zeros_like(kv_block[0]))
    return (inputs, parts, forward, backward, identity)


def finish(inputs, parts, state_in, suffix_in):
    queries, keys, values, out_grad, decay_factor = inputs
    factor, kv_block, qo_block, rising, keep, local_q, local_k, local_v = parts
    blocks = factor.shape[0]
    states = [state_in]
    index = 0
    states.append(factor[index][:, None, None] * states[-1] + kv_block[index])
    suffixes = [suffix_in]
    index = 1
    suffixes.insert(0, qo_block[index] + factor[index][:, None, None] * suffixes[0])
    state_all = jnp.stack(states).astype(jnp.bfloat16)
    suffix_all = jnp.stack(suffixes).astype(jnp.bfloat16)
    grad_q = local_q + rising[..., None] * jnp.einsum(
        "nthj,nhij->nthi", out_grad, state_all, preferred_element_type=jnp.float32
    )
    grad_k = local_k + keep[..., None] * jnp.einsum(
        "nshj,nhij->nshi", values, suffix_all, preferred_element_type=jnp.float32
    )
    grad_v = local_v + keep[..., None] * jnp.einsum(
        "nshi,nhij->nshj", keys, suffix_all, preferred_element_type=jnp.float32
    )
    shape = (blocks * queries.shape[1], queries.shape[2] * queries.shape[3])
    return (
        grad_q.astype(jnp.bfloat16).reshape(shape),
        grad_k.astype(jnp.bfloat16).reshape(shape),
        grad_v.astype(jnp.bfloat16).reshape(shape),
    )


def masked(received, valid):
    return (jnp.where(valid, received[0], 1.0), jnp.where(valid, received[1], 0.0))


def doubling(own, identity):
    count = lax.axis_size("seq")
    index = lax.axis_index("seq")
    rounds = 0
    while 1 << rounds < count:
        rounds = rounds + 1
    window_up, window_down = (own[0], own[1])
    prefix, suffix = (identity, identity)
    for level in range(rounds):
        step = 1 << level
        from_lower = shifted((window_up[0], window_up[1]), "seq", step)
        from_lower = masked(from_lower, index >= step)
        from_upper = shifted((window_down[0], window_down[1]), "seq", -step)
        from_upper = masked(from_upper, index + step < count)
        prefix = chain(from_lower, prefix)
        suffix = chain(from_upper, suffix)
        window_up = chain(from_lower, window_up)
        window_down = chain(from_upper, window_down)
    return (prefix[1], suffix[1])


def per_device(queries, keys, values, out_grad, decay_log):
    moved = (
        lax.all_to_all(queries, "head", split_axis=1, concat_axis=0, tiled=True),
        lax.all_to_all(keys, "head", split_axis=1, concat_axis=0, tiled=True),
        lax.all_to_all(values, "head", split_axis=1, concat_axis=0, tiled=True),
        lax.all_to_all(out_grad, "head", split_axis=1, concat_axis=0, tiled=True),
        lax.all_to_all(decay_log, "head", split_axis=1, concat_axis=0, tiled=True),
    )
    inputs, parts, forward, backward, identity = prepare(*moved)
    state_in, suffix_in = doubling((forward, backward), identity)
    grads = finish(inputs, parts, state_in, suffix_in)
    result = (
        lax.all_to_all(grads[0], "head", split_axis=0, concat_axis=1, tiled=True),
        lax.all_to_all(grads[1], "head", split_axis=0, concat_axis=1, tiled=True),
        lax.all_to_all(grads[2], "head", split_axis=0, concat_axis=1, tiled=True),
    )
    return (result[0], result[1], result[2])


def solution(mesh):
    return jax.shard_map(
        per_device,
        mesh=mesh,
        in_specs=(
            P(("parts", "seq", "head"), None),
            P(("parts", "seq", "head"), None),
            P(("parts", "seq", "head"), None),
            P(("parts", "seq", "head"), None),
            P(("parts", "seq", "head"), None),
        ),
        out_specs=(
            P(("parts", "seq", "head"), None),
            P(("parts", "seq", "head"), None),
            P(("parts", "seq", "head"), None),
        ),
        check_vma=False,
    )
```

profile of v0, /device:TPU:25, one launch (start us, length us, event | category | flops | bytes accessed | tf_op | source)
XLA Modules:
  0.0 240.5 jit_solution(8800016637477108151)
XLA Ops:
  2.1 3.9 %all-to-all-start.2 = ((bf16[2,2,512]{2,1,0:T(2,128)(2,1)}), bf16[2,2,512]{2,1,0:T(2,128)(2,1)S(1)}, u32[]{:S(2)}, u32[]{:S(2)}) async-start(bf16[2,2,512]{2,1,0:T(2,128)(2,1)} %reshape.84), calls=%async_computation.2 | async-start | bytes 8192 | tf_op jit(solution)/shard_map/all_to_all | solution.py:134
  6.0 1.9 copy.214
  7.8 3.5 %all-to-all-start = ((bf16[64,2,2048]{2,0,1:T(8,128)(2,1)}), bf16[64,2,2048]{2,0,1:T(8,128)(2,1)S(1)}, u32[]{:S(2)}, u32[]{:S(2)}) async-start(bf16[64,2,2048]{2,0,1:T(8,128)(2,1)} %bitcast.226), calls=%async_computation | async-start | bytes 1048576 | tf_op jit(solution)/shard_map/all_to_all | solution.py:133
  13.5 4.1 %all_to_all.134 = bf16[64,2,2048]{2,0,1:T(8,128)(2,1)S(1)} all-to-all(bf16[64,2,2048]{2,0,1:T(8,128)(2,1)S(1)} %bitcast.228), channel_id=1, replica_groups=mesh['parts'=2,'seq'=8,'head'=2] {'head'}, dimensions={1} | all-to-all | bytes 1048576 | tf_op jit(solution)/shard_map/all_to_all | solution.py:130
  17.7 1.8 fusion.20
  20.6 3.0 %collective-permute-start.7 = (f32[16,128,128]{1,2,0:T(8,128)}, f32[16,128,128]{1,2,0:T(8,128)}, u32[]{:S(2)}, u32[]{:S(2)}) collective-permute-start(f32[16,128,128]{1,2,0:T(8,128)} %fusion.14), channel_id=1, source_target_pairs={{2,0},{4,2},{6,4},{8,6},{10,8},{12,10},{14,12},{3,1},{5,3},{7,5},{... | collective-permute-start | bytes 3145736 | tf_op jit(solution)/shard_map/ppermute | solution.py:12
  23.7 23.5 %collective-permute-done.7 = f32[16,128,128]{1,2,0:T(8,128)} collective-permute-done((f32[16,128,128]{1,2,0:T(8,128)}, f32[16,128,128]{1,2,0:T(8,128)}, u32[]{:S(2)}, u32[]{:S(2)}) %collective-permute-start.7) | collective-permute-done | bytes 1048608 | tf_op jit(solution)/shard_map/ppermute | solution.py:12
  47.2 2.5 %multiply_add_fusion.1 = f32[16,128,128]{1,2,0:T(8,128)} fusion(f32[16,128,128]{1,2,0:T(8,128)} %collective-permute-done.7, f32[16]{0:T(128)S(1)} %fusion.66, pred[]{:T(512)S(6)} %lt.10, f32[2,16,128,128]{2,3,1,0:T(8,128)S(1)} %fusion.20, f32[16]{0:T(128)S(1)} %get-tuple-element.13), kind=kLoop, calls=%fused_computation.36 | loop fusion | flops 1310720 | bytes 4194433 | tf_op jit(solution)/shard_map/add | solution.py:44
  49.7 3.2 %collective-permute-start.8 = (f32[16,128,128]{1,2,0:T(8,128)}, f32[16,128,128]{1,2,0:T(8,128)}, u32[]{:S(2)}, u32[]{:S(2)}) collective-permute-start(f32[16,128,128]{1,2,0:T(8,128)} %multiply_add_fusion.1), channel_id=1, source_target_pairs={{4,0},{6,2},{8,4},{10,6},{12,8},{14,10},{5,1},{7,3},{9,5},{11,7},{... | collective-permute-start | bytes 3145736 | tf_op jit(solution)/shard_map/ppermute | solution.py:12
  52.9 4.0 %collective-permute-start = (f32[16]{0:T(128)S(1)}, f32[16]{0:T(128)S(1)}, u32[]{:S(2)}, u32[]{:S(2)}) collective-permute-start(f32[16]{0:T(128)S(1)} %fusion.66), channel_id=1, source_target_pairs={{0,2},{2,4},{4,6},{6,8},{8,10},{10,12},{12,14},{1,3},{3,5},{5,7},{... | collective-permute-start | bytes 200 | tf_op jit(solution)/shard_map/ppermute | solution.py:12
  56.9 2.2 collective-permute-start.5
  59.1 14.4 %collective-permute-done.5 = f32[16]{0:T(128)S(1)} collective-permute-done((f32[16]{0:T(128)S(1)}, f32[16]{0:T(128)S(1)}, u32[]{:S(2)}, u32[]{:S(2)}) %collective-permute-start.5) | collective-permute-done | bytes 96 | tf_op jit(solution)/shard_map/ppermute | solution.py:12
  73.5 2.4 multiply_add_fusion
  75.8 5.3 %collective-permute-start.9 = (f32[16,128,128]{1,2,0:T(8,128)}, f32[16,128,128]{1,2,0:T(8,128)}, u32[]{:S(2)}, u32[]{:S(2)}) collective-permute-start(f32[16,128,128]{1,2,0:T(8,128)} %multiply_add_fusion), channel_id=1, source_target_pairs={{8,0},{10,2},{12,4},{14,6},{9,1},{11,3},{13,5},{15,7},{24,16},{26,... | collective-permute-start | bytes 3145736 | tf_op jit(solution)/shard_map/ppermute | solution.py:12
  82.0 5.9 %all-to-all-start.3 = ((bf16[64,2,2048]{2,0,1:T(8,128)(2,1)}), bf16[64,2,2048]{2,0,1:T(8,128)(2,1)S(1)}, u32[]{:S(2)}, u32[]{:S(2)}) async-start(bf16[64,2,2048]{2,0,1:T(8,128)(2,1)} %bitcast.227), calls=%async_computation.3 | async-start | bytes 1048576 | tf_op jit(solution)/shard_map/all_to_all | solution.py:131
  87.9 1.9 copy.213
  89.8 4.9 %all_to_all.135 = bf16[64,2,2048]{2,0,1:T(8,128)(2,1)S(1)} all-to-all(bf16[64,2,2048]{2,0,1:T(8,128)(2,1)} %bitcast.229), channel_id=1, replica_groups=mesh['parts'=2,'seq'=8,'head'=2] {'head'}, dimensions={1} | all-to-all | bytes 1048576 | tf_op jit(solution)/shard_map/all_to_all | solution.py:132
  95.5 2.5 %convolution_bitcast_fusion = f32[2,16,128,128]{2,3,1,0:T(8,128)} fusion(f32[2,64,16]{1,2,0:T(8,128)S(1)} %copy.98, bf16[64,2,2048]{2,0,1:T(8,128)(2,1)S(1)} %all-to-all-done.3, bf16[64,2,2048]{2,0,1:T(8,128)(2,1)S(1)} %all_to_all.135), kind=kOutput, calls=%fused_computation | convolution fusion | flops 67895296 | bytes 3153920 | tf_op jit(solution)/shard_map/nthi,nthj->nhij/dot_general | solution.py:21
  98.0 2.1 collective-permute-start.6
  100.9 3.2 %fusion.21 = (bf16[1,16,128,128]{2,3,1,0:T(8,128)(2,1)}, bf16[16,128,128]{1,2,0:T(8,128)(2,1)}, f32[16,128,128]{1,2,0:T(8,128)S(1)}) fusion(f32[2,16,128,128]{2,3,1,0:T(8,128)S(1)} %fusion.20, f32[16]{0:T(128)S(1)} %get-tuple-element.14, f32[16,128,128]{1,2,0:T(8,128)} %collective-permute-done.7, pred[]{:T(512)S(6)} %lt.10, ...), kind=kLoop, calls=%fused_computation.46 | loop fusion | flops 3407872 | bytes 8388803 | tf_op jit(solution)/shard_map/stack | solution.py:85
  104.1 3.7 %collective-permute-start.2 = (f32[16,128,128]{1,2,0:T(8,128)S(1)}, f32[16,128,128]{1,2,0:T(8,128)S(1)}, u32[]{:S(2)}, u32[]{:S(2)}) collective-permute-start(f32[16,128,128]{1,2,0:T(8,128)S(1)} %get-tuple-element.15), channel_id=1, source_target_pairs={{0,2},{2,4},{4,6},{6,8},{8,10},{10,12},{12,14},{1,3},{3,5},{5,7},{... | collective-permute-start | bytes 3145736 | tf_op jit(solution)/shard_map/ppermute | solution.py:12
  107.8 46.3 %collective-permute-done.2 = f32[16,128,128]{1,2,0:T(8,128)S(1)} collective-permute-done((f32[16,128,128]{1,2,0:T(8,128)S(1)}, f32[16,128,128]{1,2,0:T(8,128)S(1)}, u32[]{:S(2)}, u32[]{:S(2)}) %collective-permute-start.2) | collective-permute-done | bytes 1048608 | tf_op jit(solution)/shard_map/ppermute | solution.py:12
  155.6 2.4 %fusion.6 = bf16[2,16,64,64]{3,2,1,0:T(8,128)(2,1)} fusion(f32[2,16,64]{2,1,0:T(8,128)S(1)} %copy.92, pred[64,64]{1,0:T(8,128)(4,1)S(1)} %iota_compare_fusion, bf16[64,2,2048]{2,0,1:T(8,128)(2,1)} %copy-done.4, bf16[64,2,2048]{2,0,1:T(8,128)(2,1)} %copy-done.2), kind=kOutput, calls=%fused_computation.15 | convolution fusion | flops 34209792 | bytes 1323008 | tf_op jit(solution)/shard_map/nthd,nshd->nhts/dot_general | solution.py:32
  159.5 19.5 %collective-permute-done.3 = f32[16,128,128]{1,2,0:T(8,128)} collective-permute-done((f32[16,128,128]{1,2,0:T(8,128)S(1)}, f32[16,128,128]{1,2,0:T(8,128)}, u32[]{:S(2)}, u32[]{:S(2)}) %collective-permute-start.3) | collective-permute-done | bytes 1048608 | tf_op jit(solution)/shard_map/ppermute | solution.py:12
  179.0 2.4 multiply_add_fusion.2
  182.9 1.8 fusion.5
  184.7 1.9 fusion.11
  186.8 7.1 %all_to_all.136 = bf16[2,64,2048]{2,1,0:T(8,128)(2,1)S(1)} all-to-all(bf16[2,64,2048]{2,1,0:T(8,128)(2,1)S(1)} %bitcast.230), channel_id=1, replica_groups=mesh['parts'=2,'seq'=8,'head'=2] {'head'}, dimensions={0} | all-to-all | bytes 1048576 | tf_op jit(solution)/shard_map/all_to_all | solution.py:142
  195.7 4.2 %all_to_all.137 = bf16[2,64,2048]{2,1,0:T(8,128)(2,1)S(1)} all-to-all(bf16[2,64,2048]{2,1,0:T(8,128)(2,1)S(1)} %bitcast.232), channel_id=1, replica_groups=mesh['parts'=2,'seq'=8,'head'=2] {'head'}, dimensions={0} | all-to-all | bytes 1048576 | tf_op jit(solution)/shard_map/all_to_all | solution.py:141
  200.7 29.8 %collective-permute-done.4 = f32[16,128,128]{1,2,0:T(8,128)} collective-permute-done((f32[16,128,128]{1,2,0:T(8,128)}, f32[16,128,128]{1,2,0:T(8,128)}, u32[]{:S(2)}, u32[]{:S(2)}) %collective-permute-start.4) | collective-permute-done | bytes 1048608 | tf_op jit(solution)/shard_map/ppermute | solution.py:12
  230.6 1.9 convert_bitcast_fusion.1
  233.7 6.0 %all_to_all.138 = bf16[2,64,2048]{2,1,0:T(8,128)(2,1)S(1)} all-to-all(bf16[2,64,2048]{2,1,0:T(8,128)(2,1)S(1)} %bitcast.234), channel_id=1, replica_groups=mesh['parts'=2,'seq'=8,'head'=2] {'head'}, dimensions={0} | all-to-all | bytes 1048576 | tf_op jit(solution)/shard_map/all_to_all | solution.py:140
  (67 shorter events, 16.4 us)
Async XLA Ops:
  0.6 11.1 %copy-start.10 = (bf16[64,4096]{1,0:T(8,128)(2,1)S(1)}, bf16[64,4096]{1,0:T(8,128)(2,1)}, u32[]{:S(2)}) copy-start(bf16[64,4096]{1,0:T(8,128)(2,1)} %param.5) | copy-start | bytes 1572868
  2.1 5.8 %all-to-all-start.2 = ((bf16[2,2,512]{2,1,0:T(2,128)(2,1)}), bf16[2,2,512]{2,1,0:T(2,128)(2,1)S(1)}, u32[]{:S(2)}, u32[]{:S(2)}) async-start(bf16[2,2,512]{2,1,0:T(2,128)(2,1)} %reshape.84), calls=%async_computation.2 | async-start | bytes 8192 | tf_op jit(solution)/shard_map/all_to_all | solution.py:134
  7.8 4.9 %all-to-all-start = ((bf16[64,2,2048]{2,0,1:T(8,128)(2,1)}), bf16[64,2,2048]{2,0,1:T(8,128)(2,1)S(1)}, u32[]{:S(2)}, u32[]{:S(2)}) async-start(bf16[64,2,2048]{2,0,1:T(8,128)(2,1)} %bitcast.226), calls=%async_computation | async-start | bytes 1048576 | tf_op jit(solution)/shard_map/all_to_all | solution.py:133
  12.7 0.8 copy-start.2
  20.6 26.6 %collective-permute-start.7 = (f32[16,128,128]{1,2,0:T(8,128)}, f32[16,128,128]{1,2,0:T(8,128)}, u32[]{:S(2)}, u32[]{:S(2)}) collective-permute-start(f32[16,128,128]{1,2,0:T(8,128)} %fusion.14), channel_id=1, source_target_pairs={{2,0},{4,2},{6,4},{8,6},{10,8},{12,10},{14,12},{3,1},{5,3},{7,5},{... | collective-permute-start | bytes 3145736 | tf_op jit(solution)/shard_map/ppermute | solution.py:12
  49.7 31.4 %copy-start.11 = (bf16[64,4096]{1,0:T(8,128)(2,1)S(1)}, bf16[64,4096]{1,0:T(8,128)(2,1)}, u32[]{:S(2)}) copy-start(bf16[64,4096]{1,0:T(8,128)(2,1)} %param.6) | copy-start | bytes 1572868
  49.7 23.8 %collective-permute-start.8 = (f32[16,128,128]{1,2,0:T(8,128)}, f32[16,128,128]{1,2,0:T(8,128)}, u32[]{:S(2)}, u32[]{:S(2)}) collective-permute-start(f32[16,128,128]{1,2,0:T(8,128)} %multiply_add_fusion.1), channel_id=1, source_target_pairs={{4,0},{6,2},{8,4},{10,6},{12,8},{14,10},{5,1},{7,3},{9,5},{11,7},{... | collective-permute-start | bytes 3145736 | tf_op jit(solution)/shard_map/ppermute | solution.py:12
  52.9 6.2 %collective-permute-start = (f32[16]{0:T(128)S(1)}, f32[16]{0:T(128)S(1)}, u32[]{:S(2)}, u32[]{:S(2)}) collective-permute-start(f32[16]{0:T(128)S(1)} %fusion.66), channel_id=1, source_target_pairs={{0,2},{2,4},{4,6},{6,8},{8,10},{10,12},{12,14},{1,3},{3,5},{5,7},{... | collective-permute-start | bytes 200 | tf_op jit(solution)/shard_map/ppermute | solution.py:12
  56.9 16.6 %collective-permute-start.5 = (f32[16]{0:T(128)S(1)}, f32[16]{0:T(128)S(1)}, u32[]{:S(2)}, u32[]{:S(2)}) collective-permute-start(f32[16]{0:T(128)S(1)} %fusion.66), channel_id=1, source_target_pairs={{2,0},{4,2},{6,4},{8,6},{10,8},{12,10},{14,12},{3,1},{5,3},{7,5},{... | collective-permute-start | bytes 200 | tf_op jit(solution)/shard_map/ppermute | solution.py:12
  75.8 25.0 %collective-permute-start.9 = (f32[16,128,128]{1,2,0:T(8,128)}, f32[16,128,128]{1,2,0:T(8,128)}, u32[]{:S(2)}, u32[]{:S(2)}) collective-permute-start(f32[16,128,128]{1,2,0:T(8,128)} %multiply_add_fusion), channel_id=1, source_target_pairs={{8,0},{10,2},{12,4},{14,6},{9,1},{11,3},{13,5},{15,7},{24,16},{26,... | collective-permute-start | bytes 3145736 | tf_op jit(solution)/shard_map/ppermute | solution.py:12
  82.0 7.8 %all-to-all-start.3 = ((bf16[64,2,2048]{2,0,1:T(8,128)(2,1)}), bf16[64,2,2048]{2,0,1:T(8,128)(2,1)S(1)}, u32[]{:S(2)}, u32[]{:S(2)}) async-start(bf16[64,2,2048]{2,0,1:T(8,128)(2,1)} %bitcast.227), calls=%async_computation.3 | async-start | bytes 1048576 | tf_op jit(solution)/shard_map/all_to_all | solution.py:131
  94.7 0.8 copy-start.4
  98.0 2.9 %collective-permute-start.6 = (f32[16]{0:T(128)S(1)}, f32[16]{0:T(128)S(1)}, u32[]{:S(2)}, u32[]{:S(2)}) collective-permute-start(f32[16]{0:T(128)S(1)} %get-tuple-element.5), channel_id=1, source_target_pairs={{4,0},{6,2},{8,4},{10,6},{12,8},{14,10},{5,1},{7,3},{9,5},{11,7},{... | collective-permute-start | bytes 200 | tf_op jit(solution)/shard_map/ppermute | solution.py:12
  104.1 49.9 %collective-permute-start.2 = (f32[16,128,128]{1,2,0:T(8,128)S(1)}, f32[16,128,128]{1,2,0:T(8,128)S(1)}, u32[]{:S(2)}, u32[]{:S(2)}) collective-permute-start(f32[16,128,128]{1,2,0:T(8,128)S(1)} %get-tuple-element.15), channel_id=1, source_target_pairs={{0,2},{2,4},{4,6},{6,8},{8,10},{10,12},{12,14},{1,3},{3,5},{5,7},{... | collective-permute-start | bytes 3145736 | tf_op jit(solution)/shard_map/ppermute | solution.py:12
  154.2 24.8 %collective-permute-start.3 = (f32[16,128,128]{1,2,0:T(8,128)S(1)}, f32[16,128,128]{1,2,0:T(8,128)}, u32[]{:S(2)}, u32[]{:S(2)}) collective-permute-start(f32[16,128,128]{1,2,0:T(8,128)S(1)} %multiply_add_fusion.3), channel_id=1, source_target_pairs={{0,4},{2,6},{4,8},{6,10},{8,12},{10,14},{1,5},{3,7},{5,9},{7,11},{... | collective-permute-start | bytes 3145736 | tf_op jit(solution)/shard_map/ppermute | solution.py:12
  158.1 24.8 %copy-start.6 = (bf16[1,16,128,128]{2,3,1,0:T(8,128)(2,1)S(1)}, bf16[1,16,128,128]{2,3,1,0:T(8,128)(2,1)}, u32[]{:S(2)}) copy-start(bf16[1,16,128,128]{2,3,1,0:T(8,128)(2,1)} %get-tuple-element.3) | copy-start | bytes 1572868
  158.1 24.8 %copy-start.8 = (bf16[16,128,128]{1,2,0:T(8,128)(2,1)S(1)}, bf16[16,128,128]{1,2,0:T(8,128)(2,1)}, u32[]{:S(2)}) copy-start(bf16[16,128,128]{1,2,0:T(8,128)(2,1)} %get-tuple-element.4) | copy-start | bytes 1572868
  158.1 24.8 %collective-permute-start.1 = (f32[16]{0:T(128)S(1)}, f32[16]{0:T(128)S(1)}, u32[]{:S(2)}, u32[]{:S(2)}) collective-permute-start(f32[16]{0:T(128)S(1)} %get-tuple-element.16), channel_id=1, source_target_pairs={{0,4},{2,6},{4,8},{6,10},{8,12},{10,14},{1,5},{3,7},{5,9},{7,11},{... | collective-permute-start | bytes 200 | tf_op jit(solution)/shard_map/ppermute | solution.py:12
  181.4 3.3 %copy-start.3 = (bf16[64,2,2048]{2,0,1:T(8,128)(2,1)S(1)}, bf16[64,2,2048]{2,0,1:T(8,128)(2,1)}, u32[]{:S(2)}) copy-start(bf16[64,2,2048]{2,0,1:T(8,128)(2,1)} %copy-done.2) | copy-start | bytes 1572868
  181.4 49.1 %collective-permute-start.4 = (f32[16,128,128]{1,2,0:T(8,128)}, f32[16,128,128]{1,2,0:T(8,128)}, u32[]{:S(2)}, u32[]{:S(2)}) collective-permute-start(f32[16,128,128]{1,2,0:T(8,128)} %multiply_add_fusion.2), channel_id=1, source_target_pairs={{0,8},{2,10},{4,12},{6,14},{1,9},{3,11},{5,13},{7,15},{16,24},{18,... | collective-permute-start | bytes 3145736 | tf_op jit(solution)/shard_map/ppermute | solution.py:12
  186.6 8.0 %copy-start.5 = (bf16[64,2,2048]{2,0,1:T(8,128)(2,1)S(1)}, bf16[64,2,2048]{2,0,1:T(8,128)(2,1)}, u32[]{:S(2)}) copy-start(bf16[64,2,2048]{2,0,1:T(8,128)(2,1)} %copy-done.4) | copy-start | bytes 1572868
  186.6 8.0 %copy-start.7 = (bf16[1,16,128,128]{2,3,1,0:T(8,128)(2,1)S(1)}, bf16[1,16,128,128]{2,3,1,0:T(8,128)(2,1)}, u32[]{:S(2)}) copy-start(bf16[1,16,128,128]{2,3,1,0:T(8,128)(2,1)} %get-tuple-element.3) | copy-start | bytes 1572868
  186.6 8.0 %copy-start.9 = (bf16[16,128,128]{1,2,0:T(8,128)(2,1)S(1)}, bf16[16,128,128]{1,2,0:T(8,128)(2,1)}, u32[]{:S(2)}) copy-start(bf16[16,128,128]{1,2,0:T(8,128)(2,1)} %get-tuple-element.4) | copy-start | bytes 1572868
  193.8 1.4 copy-start.1
  200.7 31.8 %copy-start = (f32[2,16,128,128]{2,3,1,0:T(8,128)S(1)}, f32[2,16,128,128]{2,3,1,0:T(8,128)}, u32[]{:S(2)}) copy-start(f32[2,16,128,128]{2,3,1,0:T(8,128)} %convolution_bitcast_fusion) | copy-start | bytes 6291460
where the time goes:
time: 242 us; the launch traced here: 241 us
  waiting for transfers between devices  135 us (56%)
  starting transfers between devices  40.8 us (17%)
  blocking collectives  26.2 us (11%)
  other arithmetic  14.1 us (6%)
  matrix products  12.3 us (5%)
  local copies, waits for them, and re-layouts  10.9 us (5%)
    ppermute x10, waiting for transfers between devices, shifted(): return lax.ppermute(block, axis, route)  134 us
    ppermute x10, starting transfers between devices, shifted(): return lax.ppermute(block, axis, route)  27.5 us
    add x5, other arithmetic, chain(): later[0][..., None, None] * earlier[1] + later[1]  8.58 us
    all_to_all x1, blocking collectives, per_device(): lax.all_to_all(grads[2], 'head', split_axis=0, concat_axis=1, tiled=True)  7.06 us
    all_to_all x1, blocking collectives, per_device(): lax.all_to_all(grads[0], 'head', split_axis=0, concat_axis=1, tiled=True)  5.99 us
    all_to_all x1, starting transfers between devices, per_device(): lax.all_to_all(keys, 'head', split_axis=1, concat_axis=0, tiled=True)  5.89 us
    all_to_all x1, blocking collectives, per_device(): lax.all_to_all(values, 'head', split_axis=1, concat_axis=0, tiled=True)  4.86 us
  transfers between devices with their start and end apart: 13, of which 7 were waited for; matrix products, arithmetic and copies ran while one was open for 8% of the time, Pallas kernels for 0%

commit v1 on v0

v1 whole, which is shorter than its diff:
```python
import functools

import jax
import jax.numpy as jnp
from jax import lax
from jax.experimental import pallas as pl
from jax.experimental.pallas import tpu as pltpu
from jax.sharding import PartitionSpec as P

MESH = pl.DeviceIdType.MESH
F32 = jnp.float32
BF16 = jnp.bfloat16
NT = (((1,), (1,)), ((), ()))
NN = (((1,), (0,)), ((), ()))
TN = (((0,), (0,)), ((), ()))


def mm(a, b, dims):
    return lax.dot_general(a, b, dims, preferred_element_type=F32)


def kernel(
    sizes, q_ref, k_ref, v_ref, o_ref, dec_ref, gq_ref, gk_ref, gv_ref,
    x, dec, cum_b, cum_t, coef, kvqo, a_in, a_out, l_in, l_out, h_in, h_out, local, grads,
    in_own, in_send, in_recv, dec_own, dec_send, dec_recv,
    a_send, a_recv, l_send, l_recv, h_send, h_recv, out_own, out_send, out_recv,
):
    rows_n, cols_n, cores, heads, dh, per, pieces, lag = sizes
    chunks = heads // per
    blk = q_ref.shape[0]
    span = cores * blk
    half = heads * dh
    width = per * dh
    piece = half // pieces
    wire = a_in.dtype
    seq = lax.axis_index("seq")
    core = lax.axis_index("head")
    row, col = seq // cols_n, seq % cols_n
    group = cols_n * cores
    slot = col * cores + core
    sources = (k_ref, v_ref, q_ref, o_ref)

    def sides(d):
        rr = jnp.where(d == 0, row, rows_n - 1 - row)
        cc = jnp.where(d == 0, col, cols_n - 1 - col)
        return rr, cc, 1 - 2 * d

    def place(target):
        return {"seq": row * cols_n + target // cores, "head": target % cores}

    def columns(owner, start, size):
        return pl.ds(pl.multiple_of(owner * half + start, dh), size)

    def own_copy(a, p):
        return pltpu.make_async_copy(
            sources[a].at[:, columns(core, p * piece, piece)],
            x.at[a, core, :, columns(0, p * piece, piece)],
            in_own.at[a, p],
        )

    def in_copy(a, p, j):
        other = (core + j) % cores
        return pltpu.make_async_remote_copy(
            sources[a].at[:, columns(other, p * piece, piece)],
            x.at[a, core, :, columns(0, p * piece, piece)],
            in_send.at[j - 1, a, p], in_recv.at[j - 1, a, p],
            device_id={"head": other}, device_id_type=MESH,
        )

    def dec_copy(j):
        return pltpu.make_async_remote_copy(
            dec_ref, dec.at[slot], dec_send.at[j - 1], dec_recv.at[j - 1],
            device_id=place((slot + j) % group), device_id_type=MESH,
        )

    def hop(src, dst, send, recv, d, g, target):
        return pltpu.make_async_remote_copy(
            src.at[d, g], dst.at[d, g], send.at[d, g], recv.at[d, g],
            device_id={"seq": target}, device_id_type=MESH,
        )

    def a_copy(d, g):
        return hop(a_out, a_in, a_send, a_recv, d, g, seq + (1 - 2 * d) * cols_n)

    def l_copy(d, g):
        return hop(l_out, l_in, l_send, l_recv, d, g, seq + (1 - 2 * d))

    def h_copy(d, g, src):
        return hop(src, h_in, h_send, h_recv, d, g, seq - (1 - 2 * d))

    outs = (gq_ref, gk_ref, gv_ref)

    def out_copy(n, g):
        return pltpu.make_async_copy(
            grads.at[n, core, :, columns(0, g * width, width)],
            outs[n].at[:, columns(core, g * width, width)],
            out_own.at[n, g],
        )

    def back_copy(n, g, j):
        other = (core + j) % cores
        return pltpu.make_async_remote_copy(
            grads.at[n, other, :, columns(0, g * width, width)],
            outs[n].at[:, columns(core, g * width, width)],
            out_send.at[j - 1, n, g], out_recv.at[j - 1, n, g],
            device_id={"head": other}, device_id_type=MESH,
        )

    def head_rows(a, index):
        cut = x[a, :, :, pl.ds(pl.multiple_of(index * dh, dh), dh)]
        return cut.reshape(span, dh)

    own_dec = pltpu.make_async_copy(dec_ref, dec.at[slot], dec_own)
    own_dec.start()
    barrier = pltpu.get_barrier_semaphore()
    for j in range(1, group):
        pl.semaphore_signal(barrier, inc=1, device_id=place((slot + j) % group), device_id_type=MESH)

    @pl.when(row > 0)
    def _():
        pl.semaphore_signal(barrier, inc=1, device_id={"seq": seq - cols_n}, device_id_type=MESH)

    @pl.when(row < rows_n - 1)
    def _():
        pl.semaphore_signal(barrier, inc=1, device_id={"seq": seq + cols_n}, device_id_type=MESH)

    for p in range(pieces):
        for a in range(4):
            own_copy(a, p).start()

    for d in range(2):
        rr, cc, _ = sides(d)

        @pl.when(rr == 0)
        def _():
            a_in[d] = jnp.zeros_like(a_in[d])

        @pl.when(cc == 0)
        def _():
            l_in[d] = jnp.zeros_like(l_in[d])

        @pl.when(jnp.logical_or(cc == cols_n - 1, rr == 0))
        def _():
            h_in[d] = jnp.zeros_like(h_in[d])

    peers = group - 1 + jnp.where(row > 0, 1, 0) + jnp.where(row < rows_n - 1, 1, 0)
    pl.semaphore_wait(barrier, peers)

    for j in range(1, group):
        dec_copy(j).start()
    for p in range(pieces):
        for a in range(4):
            for j in range(1, cores):
                in_copy(a, p, j).start()
    own_dec.wait()
    for j in range(1, group):
        dec_copy(j).wait_recv()

    def mine(array, axis):
        result = lax.slice_in_dim(array, 0, heads, axis=axis)
        for j in range(1, cores):
            part = lax.slice_in_dim(array, j * heads, (j + 1) * heads, axis=axis)
            result = jnp.where(core == j, part, result)
        return result

    t_index = lax.broadcasted_iota(jnp.int32, (span, span), 0)
    s_index = lax.broadcasted_iota(jnp.int32, (span, span), 1)
    tri = jnp.where(t_index >= s_index, 1.0, 0.0).astype(BF16)
    logs = dec[pl.ds(col * cores, cores)].reshape(span, dec.shape[2])
    cum = mine(mm(tri, logs, NN), 1)
    cum_row = mine(mm(logs, tri, (((0,), (1,)), ((), ()))), 0)
    zero = jnp.zeros((1, dec.shape[2]), F32)
    before, own, after = zero, zero, zero
    for other in range(cols_n):
        total = zero
        for j in range(cores):
            total += jnp.sum(dec[other * cores + j].astype(F32), axis=0, keepdims=True)
        before += jnp.where(other < col, total, 0.0)
        own += jnp.where(other == col, total, 0.0)
        after += jnp.where(other > col, total, 0.0)
    kinds = [mine(k, 1) for k in (own, before + own + after, before, after)]
    for i in range(heads):
        cum_b[i] = jnp.broadcast_to(cum[:, i : i + 1], (span, dh))
        cum_t[i] = cum_row[i : i + 1, :]
        for n, kind in enumerate(kinds):
            coef[n, i] = jnp.exp(jnp.broadcast_to(kind[:, i : i + 1], (8, dh)))

    def rate(n, index):
        return coef[n, index, 0:1, :]

    def row_step(d, g):
        rr, cc, _ = sides(d)

        @pl.when(rr > 0)
        def _():
            a_copy(d, g).wait_recv()

        @pl.when(rr < rows_n - 1)
        def _():
            for j in range(per):
                index = g * per + j
                a = a_in[d, g, j].astype(F32)
                a_out[d, g, j] = (rate(1, index) * a + rate(3 - d, index) * kvqo[d, index]).astype(wire)
            a_copy(d, g).start()

        if cols_n > 1:

            @pl.when(cc == 0)
            def _():
                for j in range(per):
                    index = g * per + j
                    a = a_in[d, g, j].astype(F32)
                    l_out[d, g, j] = (rate(0, index) * a + kvqo[d, index]).astype(wire)
                l_copy(d, g).start()

            @pl.when(jnp.logical_and(cc == cols_n - 1, rr > 0))
            def _():
                h_copy(d, g, a_in).start()

    def col_step(d, g):
        rr, cc, _ = sides(d)
        if cols_n > 1:

            @pl.when(cc > 0)
            def _():
                l_copy(d, g).wait_recv()

        if cols_n > 2:

            @pl.when(jnp.logical_and(cc > 0, cc < cols_n - 1))
            def _():
                for j in range(per):
                    index = g * per + j
                    a = l_in[d, g, j].astype(F32) + rate(2 + d, index) * a_in[d, g, j].astype(F32)
                    l_out[d, g, j] = (rate(0, index) * a + kvqo[d, index]).astype(wire)
                l_copy(d, g).start()

        if cols_n > 1:

            @pl.when(jnp.logical_and(cc < cols_n - 1, rr > 0))
            def _():
                h_copy(d, g, h_out).wait_recv()

        if cols_n > 2:

            @pl.when(jnp.logical_and(jnp.logical_and(cc > 0, cc < cols_n - 1), rr > 0))
            def _():
                for j in range(per):
                    h_out[d, g, j] = (h_in[d, g, j].astype(F32) + a_in[d, g, j].astype(F32)).astype(wire)
                h_copy(d, g, h_out).start()

    def carried(d, g, j):
        index = g * per + j
        both = a_in[d, g, j].astype(F32) + h_in[d, g, j].astype(F32)
        return (l_in[d, g, j].astype(F32) + rate(2 + d, index) * both).astype(BF16)

    def first(g, _):
        @pl.when(g % (chunks // pieces) == 0)
        def _():
            p = g // (chunks // pieces)
            for a in range(4):
                own_copy(a, p).wait()
                for j in range(1, cores):
                    in_copy(a, p, j).wait_recv()

        for j in range(per):
            index = g * per + j
            cum_h = cum_b[index]
            keep = jnp.exp(cum_h[span - 1 : span, :] - cum_h)
            rising = jnp.exp(cum_h)
            weighted_v = (head_rows(1, index).astype(F32) * keep).astype(BF16)
            weighted_q = (head_rows(2, index).astype(F32) * rising).astype(BF16)
            kvqo[0, index] = mm(head_rows(0, index), weighted_v, TN)
            kvqo[1, index] = mm(weighted_q, head_rows(3, index), TN)
        for d in range(2):

            @pl.when(sides(d)[0] == 0)
            def _():
                row_step(d, g)

        return 0

    lax.fori_loop(0, chunks, first, 0)

    def within(g):
        lower = lax.broadcasted_iota(jnp.int32, (span, span), 0) >= lax.broadcasted_iota(
            jnp.int32, (span, span), 1
        )
        for j in range(per):
            index = g * per + j
            k, v, q, o = (head_rows(a, index) for a in range(4))
            mask = jnp.where(lower, jnp.exp(jnp.minimum(cum_b[index] - cum_t[index], 0.0)), 0.0)
            vscore = (mm(o, v, NT) * mask).astype(BF16)
            qscore = (mm(q, k, NT) * mask).astype(BF16)
            local[0, index] = mm(vscore, k, NN)
            local[1, index] = mm(vscore, q, TN)
            local[2, index] = mm(qscore, o, TN)

    def last(g):
        for d in range(2):
            col_step(d, g)
        for j in range(per):
            index = g * per + j
            state = carried(0, g, j)
            suffix = carried(1, g, j)
            cum_h = cum_b[index]
            keep = jnp.exp(cum_h[span - 1 : span, :] - cum_h)
            rising = jnp.exp(cum_h)
            found = (
                local[0, index] + rising * mm(head_rows(3, index), state, NT),
                local[1, index] + keep * mm(head_rows(1, index), suffix, NT),
                local[2, index] + keep * mm(head_rows(0, index), suffix, NN),
            )
            for n in range(3):
                place_at = pl.ds(pl.multiple_of(index * dh, dh), dh)
                grads[n, :, :, place_at] = found[n].astype(BF16).reshape(cores, blk, dh)
        for n in range(3):
            for j in range(1, cores):
                back_copy(n, g, j).start()
            out_copy(n, g).start()

    upper = jnp.where(2 * row >= rows_n, 1, 0)

    def second(g, _):
        @pl.when(g < chunks)
        def _():
            for i in range(2):
                d = (upper + i) % 2

                @pl.when(sides(d)[0] > 0)
                def _():
                    row_step(d, g)

            within(g)

        @pl.when(g >= lag)
        def _():
            last(g - lag)

        return 0

    lax.fori_loop(0, chunks + lag, second, 0)

    for j in range(1, group):
        dec_copy(j).wait_send()
    for p in range(pieces):
        for a in range(4):
            for j in range(1, cores):
                in_copy(a, p, j).wait_send()

    def close(g, _):
        for d in range(2):
            rr, cc, _ = sides(d)

            @pl.when(rr < rows_n - 1)
            def _():
                a_copy(d, g).wait_send()

            if cols_n > 1:

                @pl.when(cc < cols_n - 1)
                def _():
                    l_copy(d, g).wait_send()

                @pl.when(jnp.logical_and(cc > 0, rr > 0))
                def _():
                    h_copy(d, g, h_out).wait_send()

        for n in range(3):
            out_copy(n, g).wait()
            for j in range(1, cores):
                back_copy(n, g, j).wait_send()
                back_copy(n, g, j).wait_recv()
        return 0

    lax.fori_loop(0, chunks, close, 0)


def solution(mesh):
    count, cores = mesh.shape["seq"], mesh.shape["head"]
    cols_n = max(c for c in range(1, count + 1) if count % c == 0 and c * c <= count)
    rows_n = count // cols_n
    wire = BF16 if rows_n + cols_n <= 8 else F32

    def per_device(queries, keys, values, out_grad, decay_log):
        blk, model = queries.shape
        all_heads = decay_log.shape[1]
        heads, dh = all_heads // cores, model // all_heads
        per, pieces, lag = 2, 4, 2
        chunks = heads // per
        span, group = cores * blk, cols_n * cores
        sizes = (rows_n, cols_n, cores, heads, dh, per, pieces, lag)
        states = pltpu.VMEM((2, chunks, per, dh, dh), wire)
        pair = pltpu.SemaphoreType.DMA((2, chunks))
        return pl.pallas_call(
            functools.partial(kernel, sizes),
            out_shape=[jax.ShapeDtypeStruct((blk, model), BF16)] * 3,
            in_specs=[pl.BlockSpec(memory_space=pl.ANY)] * 5,
            out_specs=[pl.BlockSpec(memory_space=pl.ANY)] * 3,
            scratch_shapes=[
                pltpu.VMEM((4, cores, blk, heads * dh), BF16),
                pltpu.VMEM((group, blk, all_heads), BF16),
                pltpu.VMEM((heads, span, dh), F32),
                pltpu.VMEM((heads, 1, span), F32),
                pltpu.VMEM((4, heads, 8, dh), F32),
                pltpu.VMEM((2, heads, dh, dh), F32),
                states, states, states, states, states, states,
                pltpu.VMEM((3, heads, span, dh), F32),
                pltpu.VMEM((3, cores, blk, heads * dh), BF16),
                pltpu.SemaphoreType.DMA((4, pieces)),
                pltpu.SemaphoreType.DMA((cores - 1, 4, pieces)),
                pltpu.SemaphoreType.DMA((cores - 1, 4, pieces)),
                pltpu.SemaphoreType.DMA,
                pltpu.SemaphoreType.DMA((group - 1,)),
                pltpu.SemaphoreType.DMA((group - 1,)),
                pair, pair, pair, pair, pair, pair,
                pltpu.SemaphoreType.DMA((3, chunks)),
                pltpu.SemaphoreType.DMA((cores - 1, 3, chunks)),
                pltpu.SemaphoreType.DMA((cores - 1, 3, chunks)),
            ],
            compiler_params=pltpu.CompilerParams(
                collective_id=0, has_side_effects=True, vmem_limit_bytes=48 * 1024 * 1024
            ),
            cost_estimate=pl.CostEstimate(
                flops=20 * heads * span * dh * dh, bytes_accessed=14 * blk * model, transcendentals=0
            ),
        )(queries, keys, values, out_grad, decay_log)

    rows = P(("parts", "seq", "head"), None)
    return jax.shard_map(
        per_device, mesh=mesh, in_specs=(rows,) * 5, out_specs=(rows,) * 3, check_vma=False
    )
```

time: 242 us -> 61.6 us (0.25)
  the two profiles are of different devices: /device:TPU:25 before, /device:TPU:0 now
where the time goes in v1:
time: 61.6 us; the launch traced here: 61.2 us
  Pallas kernels  53.3 us (87%)
  local copies, waits for them, and re-layouts  7.33 us (12%)
  between operations  0.65 us (1%)
    pallas_call x1, Pallas kernels, per_device(): pl.pallas_call(functools.partial(kernel, sizes), out_shape=[jax.ShapeDtyp...  53.3 us
    unnamed x12, local copies, waits for them, and re-layouts  7.33 us

profile of v1, /device:TPU:0, one launch (start us, length us, event | category | flops | bytes accessed | tf_op | source)
XLA Modules:
  0.0 61.2 jit_solution(10484553028856251672)
XLA Ops:
  0.6 0.8 %copy.8.dec_ref = bf16[64,32]{1,0:T(8,128)(2,1)S(1)} copy(bf16[64,32]{0,1:T(8,128)(2,1)} %param.9) | data formatting | bytes 8192 | tf_op args[4]
  1.4 0.0 copy-start
  1.4 1.0 %copy-done = bf16[64,4096]{1,0:T(8,128)(2,1)S(1)} copy-done((bf16[64,4096]{1,0:T(8,128)(2,1)S(1)}, bf16[64,4096]{1,0:T(8,128)(2,1)}, u32[]{:S(2)}) %copy-start) | copy-done | bytes 524312
  2.5 0.0 copy-start.1
  2.5 1.0 %copy-done.1 = bf16[64,4096]{1,0:T(8,128)(2,1)S(1)} copy-done((bf16[64,4096]{1,0:T(8,128)(2,1)S(1)}, bf16[64,4096]{1,0:T(8,128)(2,1)}, u32[]{:S(2)}) %copy-start.1) | copy-done | bytes 524312
  3.5 0.0 copy-start.2
  3.5 1.0 %copy-done.2 = bf16[64,4096]{1,0:T(8,128)(2,1)S(1)} copy-done((bf16[64,4096]{1,0:T(8,128)(2,1)S(1)}, bf16[64,4096]{1,0:T(8,128)(2,1)}, u32[]{:S(2)}) %copy-start.2) | copy-done | bytes 524312
  4.5 0.0 copy-start.3
  4.6 1.0 %copy-done.3 = bf16[64,4096]{1,0:T(8,128)(2,1)S(1)} copy-done((bf16[64,4096]{1,0:T(8,128)(2,1)S(1)}, bf16[64,4096]{1,0:T(8,128)(2,1)}, u32[]{:S(2)}) %copy-start.3) | copy-done | bytes 524312
  5.6 53.3 %shard_map.76 = (bf16[64,4096]{1,0:T(8,128)(2,1)S(1)}, bf16[64,4096]{1,0:T(8,128)(2,1)S(1)}, bf16[64,4096]{1,0:T(8,128)(2,1)S(1)}) custom-call(bf16[64,4096]{1,0:T(8,128)(2,1)S(1)} %copy-done, bf16[64,4096]{1,0:T(8,128)(2,1)S(1)} %copy-done.1, bf16[64,4096]{1,0:T(8,128)(2,1)S(1)} %copy-done.2, bf16[64,4096]{1,0:T(8,128)(2,1)S(1)} %copy-done.3, ...), custom_call_target="tpu_custom_call" | custom-call | flops 671088640 | bytes 3670016 | tf_op jit(solution)/shard_map/pallas_call | solution.py:395
  58.9 0.8 %copy.12 = bf16[64,4096]{1,0:T(8,128)(2,1)} copy(bf16[64,4096]{1,0:T(8,128)(2,1)S(1)} %get-tuple-element.6) | data formatting | bytes 1048576
  59.6 0.8 %copy.13 = bf16[64,4096]{1,0:T(8,128)(2,1)} copy(bf16[64,4096]{1,0:T(8,128)(2,1)S(1)} %get-tuple-element.7) | data formatting | bytes 1048576
  60.4 0.8 %copy.14 = bf16[64,4096]{1,0:T(8,128)(2,1)} copy(bf16[64,4096]{1,0:T(8,128)(2,1)S(1)} %get-tuple-element.8) | data formatting | bytes 1048576
Async XLA Ops:
  1.4 1.0 %copy-start = (bf16[64,4096]{1,0:T(8,128)(2,1)S(1)}, bf16[64,4096]{1,0:T(8,128)(2,1)}, u32[]{:S(2)}) copy-start(bf16[64,4096]{1,0:T(8,128)(2,1)} %q_ref.1) | copy-start | bytes 1572868
  2.5 1.0 %copy-start.1 = (bf16[64,4096]{1,0:T(8,128)(2,1)S(1)}, bf16[64,4096]{1,0:T(8,128)(2,1)}, u32[]{:S(2)}) copy-start(bf16[64,4096]{1,0:T(8,128)(2,1)} %k_ref.1) | copy-start | bytes 1572868
  3.5 1.0 %copy-start.2 = (bf16[64,4096]{1,0:T(8,128)(2,1)S(1)}, bf16[64,4096]{1,0:T(8,128)(2,1)}, u32[]{:S(2)}) copy-start(bf16[64,4096]{1,0:T(8,128)(2,1)} %v_ref.1) | copy-start | bytes 1572868
  4.5 1.0 %copy-start.3 = (bf16[64,4096]{1,0:T(8,128)(2,1)S(1)}, bf16[64,4096]{1,0:T(8,128)(2,1)}, u32[]{:S(2)}) copy-start(bf16[64,4096]{1,0:T(8,128)(2,1)} %o_ref.1) | copy-start | bytes 1572868

commit v2 on v1

--- a/solution.py
+++ b/solution.py
@@ -25,8 +25,9 @@
     in_own, in_send, in_recv, dec_own, dec_send, dec_recv,
     a_send, a_recv, l_send, l_recv, h_send, h_recv, out_own, out_send, out_recv,
 ):
-    rows_n, cols_n, cores, heads, dh, per, pieces, lag = sizes
+    rows_n, cols_n, cores, heads, dh, per, pieces, behind, lag, paired = sizes
     chunks = heads // per
+    late = chunks - paired
     blk = q_ref.shape[0]
     span = cores * blk
     half = heads * dh
@@ -124,7 +125,8 @@
     def _():
         pl.semaphore_signal(barrier, inc=1, device_id={"seq": seq + cols_n}, device_id_type=MESH)
 
-    for p in range(pieces):
+    order = [(p + late * pieces // chunks) % pieces for p in range(pieces)]
+    for p in order:
         for a in range(4):
             own_copy(a, p).start()
 
@@ -141,14 +143,14 @@
 
         @pl.when(jnp.logical_or(cc == cols_n - 1, rr == 0))
         def _():
-            h_in[d] = jnp.zeros_like(h_in[d])
+            h_in[d, :late] = jnp.zeros_like(h_in[d, :late])
 
     peers = group - 1 + jnp.where(row > 0, 1, 0) + jnp.where(row < rows_n - 1, 1, 0)
     pl.semaphore_wait(barrier, peers)
 
     for j in range(1, group):
         dec_copy(j).start()
-    for p in range(pieces):
+    for p in order:
         for a in range(4):
             for j in range(1, cores):
                 in_copy(a, p, j).start()
@@ -163,30 +165,34 @@
             result = jnp.where(core == j, part, result)
         return result
 
-    t_index = lax.broadcasted_iota(jnp.int32, (span, span), 0)
-    s_index = lax.broadcasted_iota(jnp.int32, (span, span), 1)
-    tri = jnp.where(t_index >= s_index, 1.0, 0.0).astype(BF16)
-    logs = dec[pl.ds(col * cores, cores)].reshape(span, dec.shape[2])
-    cum = mine(mm(tri, logs, NN), 1)
-    cum_row = mine(mm(logs, tri, (((0,), (1,)), ((), ()))), 0)
-    zero = jnp.zeros((1, dec.shape[2]), F32)
+    cum = cum_row = 0.0
+    for j in range(cores):
+        t_index = lax.broadcasted_iota(jnp.int32, (span, blk), 0)
+        s_index = lax.broadcasted_iota(jnp.int32, (span, blk), 1) + j * blk
+        tri = jnp.where(t_index >= s_index, 1.0, 0.0).astype(BF16)
+        logs = dec[col * cores + j]
+        cum += mm(tri, logs, NT)
+        cum_row += mm(logs, tri, NT)
+    cum, cum_row = mine(cum, 1), mine(cum_row, 0)
+    ones = jnp.ones((span, blk), BF16)
+    zero = jnp.zeros((dec.shape[1], span), F32)
     before, own, after = zero, zero, zero
     for other in range(cols_n):
         total = zero
         for j in range(cores):
-            total += jnp.sum(dec[other * cores + j].astype(F32), axis=0, keepdims=True)
+            total += mm(dec[other * cores + j], ones, NT)
         before += jnp.where(other < col, total, 0.0)
         own += jnp.where(other == col, total, 0.0)
         after += jnp.where(other > col, total, 0.0)
-    kinds = [mine(k, 1) for k in (own, before + own + after, before, after)]
+    kinds = [jnp.exp(mine(k, 0)) for k in (own, before + own + after, before, after)]
     for i in range(heads):
         cum_b[i] = jnp.broadcast_to(cum[:, i : i + 1], (span, dh))
         cum_t[i] = cum_row[i : i + 1, :]
         for n, kind in enumerate(kinds):
-            coef[n, i] = jnp.exp(jnp.broadcast_to(kind[:, i : i + 1], (8, dh)))
+            coef[n, i] = kind[i : i + 1, :]
 
     def rate(n, index):
-        return coef[n, index, 0:1, :]
+        return coef[n, index]
 
     def row_step(d, g):
         rr, cc, _ = sides(d)
@@ -195,27 +201,66 @@
         def _():
             a_copy(d, g).wait_recv()
 
-        @pl.when(rr < rows_n - 1)
-        def _():
-            for j in range(per):
-                index = g * per + j
-                a = a_in[d, g, j].astype(F32)
-                a_out[d, g, j] = (rate(1, index) * a + rate(3 - d, index) * kvqo[d, index]).astype(wire)
-            a_copy(d, g).start()
-
-        if cols_n > 1:
-
-            @pl.when(cc == 0)
+        @pl.when(g < late)
+        def _():
+            @pl.when(rr < rows_n - 1)
             def _():
                 for j in range(per):
                     index = g * per + j
                     a = a_in[d, g, j].astype(F32)
-                    l_out[d, g, j] = (rate(0, index) * a + kvqo[d, index]).astype(wire)
-                l_copy(d, g).start()
-
-            @pl.when(jnp.logical_and(cc == cols_n - 1, rr > 0))
-            def _():
-                h_copy(d, g, a_in).start()
+                    a_out[d, g, j] = (rate(1, index) * a + rate(3 - d, index) * kvqo[d, index]).astype(wire)
+                a_copy(d, g).start()
+
+            if cols_n > 1:
+
+                @pl.when(cc == 0)
+                def _():
+                    for j in range(per):
+                        index = g * per + j
+                        a = a_in[d, g, j].astype(F32)
+                        l_out[d, g, j] = (rate(0, index) * a + kvqo[d, index]).astype(wire)
+                    l_copy(d, g).start()
+
+                @pl.when(jnp.logical_and(cc == cols_n - 1, rr > 0))
+                def _():
+                    h_copy(d, g, a_in).start()
+
+        if paired:
+            @pl.when(g >= late)
+            def _():
+                @pl.when(cc > 0)
+                def _():
+                    l_copy(d, g).wait_recv()
+
+                @pl.when(jnp.logical_and(cc == 0, rr < rows_n - 1))
+                def _():
+                    h_copy(d, g, h_out).wait_recv()
+
+                @pl.when(rr < rows_n - 1)
+                def _():
+                    for j in range(per):
+                        index = g * per + j
+                        met = jnp.where(
+                            cc == 0, h_in[d, g, j].astype(F32), rate(0, index) * l_in[d, g, j].astype(F32)
+                        )
+                        grown = rate(1, index) * a_in[d, g, j].astype(F32) + rate(3 - d, index) * kvqo[d, index]
+                        a_out[d, g, j] = (grown + met).astype(wire)
+                    a_copy(d, g).start()
+
+    def meet(d, g):
+        rr, cc, _ = sides(d)
+
+        @pl.when(cc == 0)
+        def _():
+            for j in range(per):
+                l_out[d, g, j] = kvqo[d, g * per + j].astype(wire)
+            l_copy(d, g).start()
+
+        @pl.when(jnp.logical_and(cc > 0, rr < rows_n - 1))
+        def _():
+            for j in range(per):
+                h_out[d, g, j] = kvqo[d, g * per + j].astype(wire)
+            h_copy(d, g, h_out).start()
 
     def col_step(d, g):
         rr, cc, _ = sides(d)
@@ -251,10 +296,12 @@
 
     def carried(d, g, j):
         index = g * per + j
-        both = a_in[d, g, j].astype(F32) + h_in[d, g, j].astype(F32)
+        both = a_in[d, g, j].astype(F32) + jnp.where(g < late, h_in[d, g, j].astype(F32), 0.0)
         return (l_in[d, g, j].astype(F32) + rate(2 + d, index) * both).astype(BF16)
 
-    def first(g, _):
+    def first(i, _):
+        g = (i + late) % chunks
+
         @pl.when(g % (chunks // pieces) == 0)
         def _():
             p = g // (chunks // pieces)
@@ -274,9 +321,15 @@
             kvqo[1, index] = mm(weighted_q, head_rows(3, index), TN)
         for d in range(2):
 
-            @pl.when(sides(d)[0] == 0)
+            @pl.when(jnp.logical_and(sides(d)[0] == 0, g < late))
             def _():
                 row_step(d, g)
+
+            if paired:
+
+                @pl.when(g >= late)
+                def _():
+                    meet(d, g)
 
         return 0
 
@@ -296,9 +349,39 @@
             local[1, index] = mm(vscore, q, TN)
             local[2, index] = mm(qscore, o, TN)
 
+    def sent(g):
+        for d in range(2):
+            rr, cc, _ = sides(d)
+
+            @pl.when(rr < rows_n - 1)
+            def _():
+                a_copy(d, g).wait_send()
+
+            if cols_n > 1:
+
+                @pl.when(cc < cols_n - 1)
+                def _():
+                    l_copy(d, g).wait_send()
+
+                @pl.when(jnp.logical_and(cc > 0, jnp.where(g < late, rr > 0, rr < rows_n - 1)))
+                def _():
+                    h_copy(d, g, h_out).wait_send()
+
+    def close(g, _):
+        for n in range(3):
+            out_copy(n, g).wait()
+            for j in range(1, cores):
+                back_copy(n, g, j).wait_send()
+                back_copy(n, g, j).wait_recv()
+        return 0
+
     def last(g):
-        for d in range(2):
-            col_step(d, g)
+        @pl.when(g < late)
+        def _():
+            for d in range(2):
+                col_step(d, g)
+
+        sent(g)
         for j in range(per):
             index = g * per + j
             state = carried(0, g, j)
@@ -319,18 +402,34 @@
                 back_copy(n, g, j).start()
             out_copy(n, g).start()
 
+        @pl.when(g >= 2)
+        def _():
+            close(g - 2, 0)
+
+    def open_chain(g, _):
+        for d in range(2):
+
+            @pl.when(sides(d)[0] == 0)
+            def _():
+                row_step(d, g)
+
+        return 0
+
+    if paired:
+        lax.fori_loop(late, chunks, open_chain, 0)
     upper = jnp.where(2 * row >= rows_n, 1, 0)
 
     def second(g, _):
+        for i in range(2):
+            d = (upper + i) % 2
+            at = g - i * behind
+
+            @pl.when(jnp.logical_and(sides(d)[0] > 0, jnp.logical_and(at >= 0, at < chunks)))
+            def _():
+                row_step(d, at)
+
         @pl.when(g < chunks)
         def _():
-            for i in range(2):
-                d = (upper + i) % 2
-
-                @pl.when(sides(d)[0] > 0)
-                def _():
-                    row_step(d, g)
-
             within(g)
 
         @pl.when(g >= lag)
@@ -338,8 +437,6 @@
             last(g - lag)
 
         return 0
-
-    lax.fori_loop(0, chunks + lag, second, 0)
 
     for j in range(1, group):
         dec_copy(j).wait_send()
@@ -347,33 +444,9 @@
         for a in range(4):
             for j in range(1, cores):
                 in_copy(a, p, j).wait_send()
-
-    def close(g, _):
-        for d in range(2):
-            rr, cc, _ = sides(d)
-
-            @pl.when(rr < rows_n - 1)
-            def _():
-                a_copy(d, g).wait_send()
-
-            if cols_n > 1:
-
-                @pl.when(cc < cols_n - 1)
-                def _():
-                    l_copy(d, g).wait_send()
-
-                @pl.when(jnp.logical_and(cc > 0, rr > 0))
-                def _():
-                    h_copy(d, g, h_out).wait_send()
-
-        for n in range(3):
-            out_copy(n, g).wait()
-            for j in range(1, cores):
-                back_copy(n, g, j).wait_send()
-                back_copy(n, g, j).wait_recv()
-        return 0
-
-    lax.fori_loop(0, chunks, close, 0)
+    lax.fori_loop(0, chunks + lag, second, 0)
+
+    lax.fori_loop(jnp.maximum(chunks - 2, 0), chunks, close, 0)
 
 
 def solution(mesh):
@@ -386,10 +459,11 @@
         blk, model = queries.shape
         all_heads = decay_log.shape[1]
         heads, dh = all_heads // cores, model // all_heads
-        per, pieces, lag = 2, 4, 2
+        per, pieces, behind, lag = 2, 4, 2, 8
+        paired = 2 if cols_n == 2 else 0
         chunks = heads // per
         span, group = cores * blk, cols_n * cores
-        sizes = (rows_n, cols_n, cores, heads, dh, per, pieces, lag)
+        sizes = (rows_n, cols_n, cores, heads, dh, per, pieces, behind, lag, paired)
         states = pltpu.VMEM((2, chunks, per, dh, dh), wire)
         pair = pltpu.SemaphoreType.DMA((2, chunks))
         return pl.pallas_call(
@@ -399,10 +473,10 @@
             out_specs=[pl.BlockSpec(memory_space=pl.ANY)] * 3,
             scratch_shapes=[
                 pltpu.VMEM((4, cores, blk, heads * dh), BF16),
-                pltpu.VMEM((group, blk, all_heads), BF16),
+                pltpu.VMEM((group, all_heads, blk), BF16),
                 pltpu.VMEM((heads, span, dh), F32),
                 pltpu.VMEM((heads, 1, span), F32),
-                pltpu.VMEM((4, heads, 8, dh), F32),
+                pltpu.VMEM((4, heads, 1, span), F32),
                 pltpu.VMEM((2, heads, dh, dh), F32),
                 states, states, states, states, states, states,
                 pltpu.VMEM((3, heads, span, dh), F32),
@@ -419,12 +493,12 @@
                 pltpu.SemaphoreType.DMA((cores - 1, 3, chunks)),
             ],
             compiler_params=pltpu.CompilerParams(
-                collective_id=0, has_side_effects=True, vmem_limit_bytes=48 * 1024 * 1024
+                collective_id=0, has_side_effects=True, vmem_limit_bytes=63 * 1024 * 1024
             ),
             cost_estimate=pl.CostEstimate(
                 flops=20 * heads * span * dh * dh, bytes_accessed=14 * blk * model, transcendentals=0
             ),
-        )(queries, keys, values, out_grad, decay_log)
+        )(queries, keys, values, out_grad, decay_log.T)
 
     rows = P(("parts", "seq", "head"), None)
     return jax.shard_map(

time: 61.6 us -> 39.9 us (0.65)
  Pallas kernels: 53.3 us -> 35.1 us
  local copies, waits for them, and re-layouts: 7.33 us -> 3.95 us
    pallas_call x1, Pallas kernels: 53.3 us -> 35.1 us  [per_device(): pl.pallas_call(functools.partial(kernel, sizes), out_shape=[jax.ShapeDtyp...]
    unnamed x12 -> x7, local copies, waits for them, and re-layouts: 7.33 us -> 3.95 us
where the time goes in v2:
time: 39.9 us; the launch traced here: 39.7 us
  Pallas kernels  35.1 us (88%)
  local copies, waits for them, and re-layouts  3.95 us (10%)
  between operations  0.65 us (2%)
    pallas_call x1, Pallas kernels, per_device(): pl.pallas_call(functools.partial(kernel, sizes), out_shape=[jax.ShapeDtyp...  35.1 us
    unnamed x7, local copies, waits for them, and re-layouts  3.95 us

profile of v2, /device:TPU:0, one launch (start us, length us, event | category | flops | bytes accessed | tf_op | source)
XLA Modules:
  0.0 39.7 jit_solution(1023109911204998284)
XLA Ops:
  0.6 35.1 %shard_map.76 = (bf16[64,4096]{1,0:T(8,128)(2,1)}, bf16[64,4096]{1,0:T(8,128)(2,1)}, bf16[64,4096]{1,0:T(8,128)(2,1)}) custom-call(bf16[64,4096]{1,0:T(8,128)(2,1)} %q_ref.1, bf16[64,4096]{1,0:T(8,128)(2,1)} %k_ref.1, bf16[64,4096]{1,0:T(8,128)(2,1)} %v_ref.1, bf16[64,4096]{1,0:T(8,128)(2,1)} %o_ref.1, bf16[32,64]{1,0:T(8,128)(2,1)} %bitcast.1), custom_call_target="tpu_custom_call" | custom-call | flops 671088640 | bytes 3670016 | tf_op jit(solution)/shard_map/pallas_call | solution.py:469
  35.7 0.0 copy-start.1
  35.7 1.9 %copy.11 = bf16[64,4096]{1,0:T(8,128)(2,1)} copy(bf16[64,4096]{1,0:T(8,128)(2,1)} %get-tuple-element.6) | data formatting | bytes 1048576
  37.7 0.0 copy-done.1
  37.7 0.0 copy-start
  37.7 0.8 %copy.12 = bf16[64,4096]{1,0:T(8,128)(2,1)} copy(bf16[64,4096]{1,0:T(8,128)(2,1)S(1)} %copy-done.1) | data formatting | bytes 1048576
  38.5 0.4 %copy-done = bf16[64,4096]{1,0:T(8,128)(2,1)S(1)} copy-done((bf16[64,4096]{1,0:T(8,128)(2,1)S(1)}, bf16[64,4096]{1,0:T(8,128)(2,1)}, u32[]{:S(2)}) %copy-start) | copy-done | bytes 524312
  38.9 0.8 %copy.13 = bf16[64,4096]{1,0:T(8,128)(2,1)} copy(bf16[64,4096]{1,0:T(8,128)(2,1)S(1)} %copy-done) | data formatting | bytes 1048576
Async XLA Ops:
  35.7 1.9 %copy-start.1 = (bf16[64,4096]{1,0:T(8,128)(2,1)S(1)}, bf16[64,4096]{1,0:T(8,128)(2,1)}, u32[]{:S(2)}) copy-start(bf16[64,4096]{1,0:T(8,128)(2,1)} %get-tuple-element.7) | copy-start | bytes 1572868
  37.7 1.2 %copy-start = (bf16[64,4096]{1,0:T(8,128)(2,1)S(1)}, bf16[64,4096]{1,0:T(8,128)(2,1)}, u32[]{:S(2)}) copy-start(bf16[64,4096]{1,0:T(8,128)(2,1)} %get-tuple-element.8) | copy-start | bytes 1572868

commit v3 on v2

--- a/solution.py
+++ b/solution.py
@@ -21,13 +21,14 @@
 
 def kernel(
     sizes, q_ref, k_ref, v_ref, o_ref, dec_ref, gq_ref, gk_ref, gv_ref,
-    x, dec, cum_b, cum_t, coef, kvqo, a_in, a_out, l_in, l_out, h_in, h_out, local, grads,
+    x, dec, cum_b, cum_t, rise, kept, coef, kvqo, a_in, a_out, l_in, l_out, h_in, h_out, local, grads,
     in_own, in_send, in_recv, dec_own, dec_send, dec_recv,
     a_send, a_recv, l_send, l_recv, h_send, h_recv, out_own, out_send, out_recv,
 ):
     rows_n, cols_n, cores, heads, dh, per, pieces, behind, lag, paired = sizes
     chunks = heads // per
     late = chunks - paired
+    joint = 2 if chunks % 2 == 0 else 1
     blk = q_ref.shape[0]
     span = cores * blk
     half = heads * dh
@@ -93,16 +94,16 @@
 
     def out_copy(n, g):
         return pltpu.make_async_copy(
-            grads.at[n, core, :, columns(0, g * width, width)],
-            outs[n].at[:, columns(core, g * width, width)],
+            grads.at[n, core, :, columns(0, g * joint * width, joint * width)],
+            outs[n].at[:, columns(core, g * joint * width, joint * width)],
             out_own.at[n, g],
         )
 
     def back_copy(n, g, j):
         other = (core + j) % cores
         return pltpu.make_async_remote_copy(
-            grads.at[n, other, :, columns(0, g * width, width)],
-            outs[n].at[:, columns(core, g * width, width)],
+            grads.at[n, other, :, columns(0, g * joint * width, joint * width)],
+            outs[n].at[:, columns(core, g * joint * width, joint * width)],
             out_send.at[j - 1, n, g], out_recv.at[j - 1, n, g],
             device_id={"head": other}, device_id_type=MESH,
         )
@@ -315,6 +316,8 @@
             cum_h = cum_b[index]
             keep = jnp.exp(cum_h[span - 1 : span, :] - cum_h)
             rising = jnp.exp(cum_h)
+            rise[index] = rising
+            kept[index] = keep
             weighted_v = (head_rows(1, index).astype(F32) * keep).astype(BF16)
             weighted_q = (head_rows(2, index).astype(F32) * rising).astype(BF16)
             kvqo[0, index] = mm(head_rows(0, index), weighted_v, TN)
@@ -386,9 +389,7 @@
             index = g * per + j
             state = carried(0, g, j)
             suffix = carried(1, g, j)
-            cum_h = cum_b[index]
-            keep = jnp.exp(cum_h[span - 1 : span, :] - cum_h)
-            rising = jnp.exp(cum_h)
+            rising, keep = rise[index], kept[index]
             found = (
                 local[0, index] + rising * mm(head_rows(3, index), state, NT),
                 local[1, index] + keep * mm(head_rows(1, index), suffix, NT),
@@ -397,14 +398,17 @@
             for n in range(3):
                 place_at = pl.ds(pl.multiple_of(index * dh, dh), dh)
                 grads[n, :, :, place_at] = found[n].astype(BF16).reshape(cores, blk, dh)
-        for n in range(3):
-            for j in range(1, cores):
-                back_copy(n, g, j).start()
-            out_copy(n, g).start()
-
-        @pl.when(g >= 2)
-        def _():
-            close(g - 2, 0)
+        @pl.when(g % joint == joint - 1)
+        def _():
+            pair = g // joint
+            for n in range(3):
+                for j in range(1, cores):
+                    back_copy(n, pair, j).start()
+                out_copy(n, pair).start()
+
+            @pl.when(pair >= 1)
+            def _():
+                close(pair - 1, 0)
 
     def open_chain(g, _):
         for d in range(2):
@@ -446,7 +450,7 @@
                 in_copy(a, p, j).wait_send()
     lax.fori_loop(0, chunks + lag, second, 0)
 
-    lax.fori_loop(jnp.maximum(chunks - 2, 0), chunks, close, 0)
+    close(chunks // joint - 1, 0)
 
 
 def solution(mesh):
@@ -476,6 +480,8 @@
                 pltpu.VMEM((group, all_heads, blk), BF16),
                 pltpu.VMEM((heads, span, dh), F32),
                 pltpu.VMEM((heads, 1, span), F32),
+                pltpu.VMEM((heads, span, dh), F32),
+                pltpu.VMEM((heads, span, dh), F32),
                 pltpu.VMEM((4, heads, 1, span), F32),
                 pltpu.VMEM((2, heads, dh, dh), F32),
                 states, states, states, states, states, states,

time: 39.9 us -> 39.8 us (level)
  no operation moved by 1% of the time
where the time goes in v3:
time: 39.8 us; the launch traced here: 39.6 us
  Pallas kernels  35 us (88%)
  local copies, waits for them, and re-layouts  3.95 us (10%)
  between operations  0.65 us (2%)
    pallas_call x1, Pallas kernels, per_device(): pl.pallas_call(functools.partial(kernel, sizes), out_shape=[jax.ShapeDtyp...  35 us
    unnamed x7, local copies, waits for them, and re-layouts  3.95 us

profile of v3, /device:TPU:0, one launch (start us, length us, event | category | flops | bytes accessed | tf_op | source)
XLA Modules:
  0.0 39.6 jit_solution(6858443872228955812)
XLA Ops:
  0.6 35.0 %shard_map.76 = (bf16[64,4096]{1,0:T(8,128)(2,1)}, bf16[64,4096]{1,0:T(8,128)(2,1)}, bf16[64,4096]{1,0:T(8,128)(2,1)}) custom-call(bf16[64,4096]{1,0:T(8,128)(2,1)} %q_ref.1, bf16[64,4096]{1,0:T(8,128)(2,1)} %k_ref.1, bf16[64,4096]{1,0:T(8,128)(2,1)} %v_ref.1, bf16[64,4096]{1,0:T(8,128)(2,1)} %o_ref.1, bf16[32,64]{1,0:T(8,128)(2,1)} %bitcast.1), custom_call_target="tpu_custom_call" | custom-call | flops 671088640 | bytes 3670016 | tf_op jit(solution)/shard_map/pallas_call | solution.py:473
  35.7 0.0 copy-start.1
  35.7 1.9 %copy.11 = bf16[64,4096]{1,0:T(8,128)(2,1)} copy(bf16[64,4096]{1,0:T(8,128)(2,1)} %get-tuple-element.6) | data formatting | bytes 1048576
  37.6 0.0 copy-done.1
  37.6 0.0 copy-start
  37.6 0.8 %copy.12 = bf16[64,4096]{1,0:T(8,128)(2,1)} copy(bf16[64,4096]{1,0:T(8,128)(2,1)S(1)} %copy-done.1) | data formatting | bytes 1048576
  38.4 0.4 %copy-done = bf16[64,4096]{1,0:T(8,128)(2,1)S(1)} copy-done((bf16[64,4096]{1,0:T(8,128)(2,1)S(1)}, bf16[64,4096]{1,0:T(8,128)(2,1)}, u32[]{:S(2)}) %copy-start) | copy-done | bytes 524312
  38.8 0.8 %copy.13 = bf16[64,4096]{1,0:T(8,128)(2,1)} copy(bf16[64,4096]{1,0:T(8,128)(2,1)S(1)} %copy-done) | data formatting | bytes 1048576
Async XLA Ops:
  35.7 1.9 %copy-start.1 = (bf16[64,4096]{1,0:T(8,128)(2,1)S(1)}, bf16[64,4096]{1,0:T(8,128)(2,1)}, u32[]{:S(2)}) copy-start(bf16[64,4096]{1,0:T(8,128)(2,1)} %get-tuple-element.7) | copy-start | bytes 1572868
  37.6 1.2 %copy-start = (bf16[64,4096]{1,0:T(8,128)(2,1)S(1)}, bf16[64,4096]{1,0:T(8,128)(2,1)}, u32[]{:S(2)}) copy-start(bf16[64,4096]{1,0:T(8,128)(2,1)} %get-tuple-element.8) | copy-start | bytes 1572868
